TPU v7x, 32 devices: a whole 2x2x4 slice. The times are simulated.
32 devices in a mesh: blk: 8 (over z, y), head: 2 (over x), batch: 2 (over core).
Axes of the slice: x: 2, y: 2, z: 4, core: 2. Of those that a mesh axis runs over, the one named last changes fastest.
Arguments:
- query_rows: bfloat16 [4096, 3072], P(('batch', 'blk', 'head')), parts along dimension 0, may hold values from -16 to 16
- key_rows: bfloat16 [4096, 3072], P(('batch', 'blk', 'head')), parts along dimension 0, may hold values from -16 to 16
- value_rows: bfloat16 [4096, 3072], P(('batch', 'blk', 'head')), parts along dimension 0, may hold values from -6 to 6
- q_gain: float32 [3072], replicated, may hold values from 1 to 3
- k_gain: float32 [3072], replicated, may hold values from 1 to 3
- tile_mask: int32 [16, 16], replicated, may hold values from 0 to 1, as said below
Outputs:
- attended: bfloat16 [4096, 3072], P(('batch', 'blk', 'head')), parts along dimension 0
There are 2 independent parts, one for each index of `batch`. A program takes and returns all parts, laid end to end along the dimension named above; an argument that names none is the same for every part. Nothing has to cross between parts.
Inputs may be any that keep to these rules, and one draw needn't show every extreme that they name: `tile_mask`: 1 where a block of 128 query positions may attend to a block of 128 key positions; the main diagonal and the two beside it are always 1.
All inputs are finite; a program needn't handle non-finite values.
Results may differ from a plain program's by a relative error of at most 0.012.
The roundings to bfloat16 on the way count: a program that leaves them out, or rounds other values in their place, can miss the bound.
Values may be sent and summed in bfloat16 or wider, within the bound.
No kernel may reach another device: no remote copies, remote signals or barrier semaphores. Data moves between devices by JAX's collectives and lax.ppermute only.
A program may use at most 128 MiB of HBM per device.

v0:
```python
import functools

import jax
import jax.numpy as jnp
from jax import lax
from jax.experimental import pallas as pl
from jax.experimental.pallas import tpu as pltpu
from jax.sharding import Mesh, PartitionSpec as P

HEADS = 24
HDIM = 128
TILE = 128
EPS = 1e-06
MASKED = -1e30
NEAR = ("outer", "head")
FAR = ("outer", "inner", "head")
PARAMS = pltpu.CompilerParams(vmem_limit_bytes=48 * 1024 * 1024)
PACK_PARAMS = pltpu.CompilerParams(vmem_limit_bytes=61 * 1024 * 1024)
BF16 = jnp.bfloat16
SHARED_COST = 24 * 2**30
SCALE = 1.4426950408889634 * HDIM ** (-0.5)


def shape(*dims):
    return jax.ShapeDtypeStruct(dims, BF16)


def exchange(x, axes):
    return lax.all_to_all(x, axes, split_axis=0, concat_axis=0, tiled=True)


def pack_kernel(store, send, inputs, outputs, scratch):
    q_hbm, k_hbm, v_hbm, qg_hbm, kg_hbm = inputs
    q_in, k_in, v_in, qg, kg, sems, *kept = scratch
    copies = [
        pltpu.make_async_copy(src, dst, sems.at[n])
        for n, (src, dst) in enumerate(
            ((v_hbm, v_in), (q_hbm, q_in), (qg_hbm, qg), (k_hbm, k_in), (kg_hbm, kg))
        )
    ]
    for copy in copies:
        copy.start()

    group = 16

    def normalize(block, gain):
        widened = block.astype(jnp.float32)
        mean_square = jnp.mean(widened * widened, axis=-1, keepdims=True)
        return (widened * lax.rsqrt(mean_square + EPS) * gain[...]).astype(BF16)

    sent = []
    for first, which, ref, gain in ((0, 2, v_in, None), (1, 0, q_in, qg), (3, 1, k_in, kg)):
        copies[first].wait()
        if gain is not None:
            copies[first + 1].wait()
        for row in range(0, ref.shape[0], group):
            at = slice(row, row + group)
            store(which, at, ref[at] if gain is None else normalize(ref[at], gain), kept)
        sent += send(which, outputs, kept)
    for copy in sent:
        copy.wait()


def pack(store, send, out_shape, rows, features, arrays, kept=()):
    q, k, v, q_gain, k_gain = arrays
    hbm = pl.BlockSpec(memory_space=pltpu.HBM)

    def kernel(*refs):
        pack_kernel(store, send, refs[:5], refs[5 : 5 + len(out_shape)], refs[5 + len(out_shape) :])

    return pl.pallas_call(
        kernel,
        in_specs=[hbm] * 5,
        out_specs=[hbm] * len(out_shape),
        out_shape=out_shape,
        scratch_shapes=[pltpu.VMEM((rows, features), BF16)] * 3
        + [pltpu.VMEM((1, features), jnp.float32)] * 2
        + [pltpu.SemaphoreType.DMA((5,)), *kept],
        compiler_params=PACK_PARAMS,
        name="pack",
    )(q, k, v, q_gain.reshape(1, -1), k_gain.reshape(1, -1))


def first_pass(query, key, bias_at, scores_ref, c, largest):
    s = lax.dot_general(key, query, (((1,), (1,)), ((), ())), preferred_element_type=jnp.float32)
    scores_ref[c] = s
    for t in range(key.shape[0] // TILE):
        tile = s[t * TILE : (t + 1) * TILE].reshape(TILE // 8, 8, -1)
        largest = jnp.maximum(largest, jnp.max(tile, axis=0) + bias_at(t))
    return largest


def second_pass(scores_ref, c, col_max, bias_at, value_t, state):
    total, mixed = state
    wide, bm = scores_ref.shape[1:]
    weights = []
    for t in range(wide // TILE):
        tile = scores_ref[c, t * TILE : (t + 1) * TILE].reshape(TILE // 8, 8, bm)
        tile = jnp.exp2(tile * SCALE - (col_max - bias_at(t))[None])
        total = total + jnp.sum(tile, axis=0)
        weights.append(tile.reshape(TILE, bm).astype(BF16))
    weights = jnp.concatenate(weights, axis=0)
    return total, mixed + jnp.dot(value_t, weights, preferred_element_type=jnp.float32)


def over_all(largest):
    return jnp.broadcast_to(jnp.max(largest, axis=0, keepdims=True) * SCALE, largest.shape)


def divide(total, mixed):
    return (mixed / jnp.sum(total, axis=0, keepdims=True)).T.astype(BF16)


def bias_of(band, bm, live_at):
    lane = lax.broadcasted_iota(jnp.int32, (8, bm), 1)
    bias = jnp.zeros((8, bm), jnp.float32)
    for a in range(bm // band):
        dead = jnp.where(live_at(a), 0.0, MASKED).astype(jnp.float32)
        bias = jnp.where((lane >= a * band) & (lane < (a + 1) * band), dead, bias)
    return bias


def attend(query, band, key_at, value_at, key_blocks, live_at, scores_ref):
    wide, bm = scores_ref.shape[1:]

    def bias_at(c):
        return lambda t: bias_of(band, bm, lambda a: live_at(a, c * (wide // TILE) + t))

    def score(c, largest):
        return first_pass(query, key_at(c), bias_at(c), scores_ref, c, largest)

    largest = lax.fori_loop(0, key_blocks, score, jnp.full((8, bm), MASKED, jnp.float32))
    col_max = over_all(largest)

    def mix(c, state):
        return second_pass(scores_ref, c, col_max, bias_at(c), transposed(value_at(c)), state)

    state = jnp.zeros((8, bm), jnp.float32), jnp.zeros((HDIM, bm), jnp.float32)
    return divide(*lax.fori_loop(0, key_blocks, mix, state))


def transposed(block):
    return block.astype(jnp.float32).T.astype(BF16)


def attend_blocks(blocks, band, query_at, key_at, value_t, key_blocks, live_at, finish, scores):
    wide, bm = scores[0].shape[1:]
    empty = jnp.full((8, bm), MASKED, jnp.float32)
    nothing = jnp.zeros((8, bm), jnp.float32), jnp.zeros((HDIM, bm), jnp.float32)

    def bias_at(i, c):
        return lambda t: bias_of(band, bm, lambda a: live_at(i, a, c, t))

    def both(i, col_max, now, following):
        later = jnp.minimum(i + 1, blocks - 1)
        query = query_at(later)
        largest, state = empty, nothing
        for c in range(key_blocks):
            largest = first_pass(query, key_at(c), bias_at(later, c), following, c, largest)
            state = second_pass(now, c, col_max, bias_at(i, c), value_t[:, c * wide : (c + 1) * wide], state)
        finish(i, divide(*state))
        return over_all(largest)

    largest = empty
    query = query_at(0)
    for c in range(key_blocks):
        largest = first_pass(query, key_at(c), bias_at(0, c), scores[0], c, largest)

    def pair(n, col_max):
        col_max = both(2 * n, col_max, scores[0], scores[1])
        return both(2 * n + 1, col_max, scores[1], scores[0])

    lax.fori_loop(0, blocks // 2, pair, over_all(largest))


def partner(me, step):
    first, second = step
    return me ^ jnp.where(lax.axis_index("batch") == 0, first, second)


def collect_kernel(steps, rows, *refs):
    pieces, (q_out, kv_out) = refs[:-2], refs[-2:]
    me = lax.axis_index(NEAR)
    for step, piece in zip(steps, pieces):
        at = pl.ds(pl.multiple_of(partner(me, step) * rows, rows), rows)
        q_out[at] = piece[0]
        kv_out[:, at] = piece[1:]


def shared_kernel(mask_ref, q_ref, own_ref, other_ref, out_ref, value_t, *scores):
    mine = lax.axis_index("inner")
    _, wide, bm = scores[0].shape
    blocks = q_ref.shape[0] // wide

    def key_at(c):
        ref = own_ref if c < blocks else other_ref
        return ref[0, c % blocks * wide : (c % blocks + 1) * wide]

    for n, ref in enumerate((own_ref, other_ref)):
        for t in range(blocks * wide // TILE):
            at = (n * blocks * wide) + t * TILE
            value_t[:, at : at + TILE] = transposed(ref[1, t * TILE : (t + 1) * TILE])

    def tile(block, inner, t):
        return (block * 2 + inner) * (wide // TILE) + t

    def finish(i, mixed):
        out_ref[pl.ds(pl.multiple_of(i * bm, bm), bm)] = mixed

    attend_blocks(
        blocks,
        TILE,
        lambda i: q_ref[pl.ds(pl.multiple_of(i * bm, bm), bm)],
        key_at,
        value_t,
        2 * blocks,
        lambda i, a, c, t: mask_ref[tile(i, mine, a), tile(c % blocks, mine if c < blocks else 1 - mine, t)] != 0,
        finish,
        scores,
    )


def whole_kernel(sources, mask_ref, qkv_ref, *refs):
    out_ref, value_t, *scores = refs[-4:]
    rows = qkv_ref.shape[2]
    _, wide, bm = scores[0].shape
    bands, tiles = bm // rows, wide // TILE
    for t in range(sources):
        value_t[:, t * TILE : (t + 1) * TILE] = transposed(qkv_ref[t, 2])

    def finish(i, mixed):
        out_ref[pl.ds(i * bands, bands)] = mixed.reshape(bands, rows, HDIM)

    attend_blocks(
        sources // bands,
        rows,
        lambda i: qkv_ref[pl.ds(i * bands, bands), 0].reshape(bm, HDIM),
        lambda c: qkv_ref[c * tiles : (c + 1) * tiles, 1].reshape(wide, HDIM),
        value_t,
        sources // tiles,
        lambda i, a, c, t: mask_ref[i * bands + a, c * tiles + t] != 0,
        finish,
        scores,
    )


def halved(far, near):
    steps = []
    for d in reversed(range(near // 2)):
        steps += [(near // 2 + d, d), (d, near // 2 + d)]

    def swap(piece, step):
        pairs = [(2 * i + b, 2 * (i ^ step[b]) + b) for i in range(near) for b in range(2)]
        return lax.ppermute(piece, (*NEAR, "batch"), pairs)

    def per_device(query_rows, key_rows, value_rows, q_gain, k_gain, tile_mask):
        rows, features = query_rows.shape

        def store(which, at, block, kept):
            near_heads, far_heads = kept[:2]
            for h in range(near):
                near_heads[h, which, at] = block[:, h * HDIM : (h + 1) * HDIM]
            for h in range(far):
                far_heads[h, which, at] = block[:, (near + h) * HDIM : (near + h + 1) * HDIM]

        def send(which, outs, kept):
            near_heads, far_heads, near_sems, far_sems = kept
            me = lax.axis_index(NEAR)
            copies = [
                pltpu.make_async_copy(near_heads.at[partner(me, step), which], outs[n].at[which], near_sems.at[which, n])
                for n, step in enumerate(steps)
            ]
            copies.append(pltpu.make_async_copy(far_heads.at[:, which], outs[-1].at[:, which], far_sems.at[which]))
            for copy in copies:
                copy.start()
            return copies

        def read(shared, whole, out_ref):
            for d in range(near):
                out_ref[:, d * HDIM : (d + 1) * HDIM] = shared[d]
            for d in range(far):
                out_ref[:, (near + d) * HDIM : (near + d + 1) * HDIM] = whole[d]

        *shared, whole = pack(
            store,
            send,
            [shape(3, rows, HDIM)] * near + [shape(far, 3, rows, HDIM)],
            rows,
            features,
            (query_rows, key_rows, value_rows, q_gain, k_gain),
            [
                pltpu.VMEM((near, 3, rows, HDIM), BF16),
                pltpu.VMEM((far, 3, rows, HDIM), BF16),
                pltpu.SemaphoreType.DMA((3, near)),
                pltpu.SemaphoreType.DMA((3,)),
            ],
        )
        shared = [swap(piece, step) for step, piece in zip(steps, shared)]
        whole = exchange(whole, FAR)
        q_near, kv_near = pl.pallas_call(
            functools.partial(collect_kernel, steps, rows),
            out_shape=[shape(near * rows, HDIM), shape(2, near * rows, HDIM)],
            compiler_params=PARAMS,
            name="collect",
        )(*shared)
        kv_other = lax.ppermute(kv_near, "inner", [(0, 1), (1, 0)])

        wide = 2 * TILE
        blocks = far * rows // wide
        smem, vmem = pl.BlockSpec(memory_space=pltpu.SMEM), pl.BlockSpec(memory_space=pltpu.VMEM)
        scratch = [pltpu.VMEM((HDIM, far * rows), BF16)]
        scores = [pltpu.VMEM((blocks, wide, wide), jnp.float32)] * 2
        shared = pl.pallas_call(
            shared_kernel,
            in_specs=[smem] + [vmem] * 3,
            out_shape=shape(near * rows, HDIM),
            scratch_shapes=scratch + scores,
            compiler_params=PARAMS,
            cost_estimate=pl.CostEstimate(flops=SHARED_COST, bytes_accessed=2**21, transcendentals=0),
            name="attend_shared",
        )(tile_mask, q_near, kv_near, kv_other)

        whole = pl.pallas_call(
            functools.partial(whole_kernel, far),
            in_specs=[smem, vmem, pl.BlockSpec(memory_space=pl.ANY)],
            out_shape=shape(far, rows, HDIM),
            scratch_shapes=scratch + [pltpu.VMEM((blocks // 2, 2 * wide, wide), jnp.float32)] * 2,
            compiler_params=PARAMS,
            cost_estimate=pl.CostEstimate(flops=2**33, bytes_accessed=2**22, transcendentals=0),
            name="attend_whole",
        )(tile_mask, whole, shared)
        shared = exchange(shared.reshape(near, rows, HDIM), NEAR)
        return pl.pallas_call(
            read, out_shape=shape(rows, features), compiler_params=PARAMS, name="unpack"
        )(shared, exchange(whole, FAR))

    return per_device


def gathered_kernel(outer, inner, mask_ref, q_ref, kv_ref, out_ref, scores_ref):
    i = pl.program_id(0)
    block = out_ref.shape[0] * out_ref.shape[1] * out_ref.shape[2]
    tiles = block // TILE
    q_tile = (i * inner + lax.axis_index("inner")) * tiles
    mixed = attend(
        q_ref[0, :, 0].reshape(block, HDIM),
        TILE,
        lambda c: kv_ref[lax.rem(c, inner), lax.div(c, inner), :, 1].reshape(block, HDIM),
        lambda c: kv_ref[lax.rem(c, inner), lax.div(c, inner), :, 2].reshape(block, HDIM),
        outer * inner,
        lambda a, t: mask_ref[q_tile + a, t] != 0,
        scores_ref,
    )
    out_ref[...] = mixed.reshape(out_ref.shape)


def gathered(outer, inner, n_head, near):
    width = HEADS // near * HDIM

    def per_device(query_rows, key_rows, value_rows, q_gain, k_gain, tile_mask):
        rows, features = query_rows.shape
        block = rows * n_head

        def store(which, at, block, kept):
            for d in range(near):
                kept[0][d, which, at] = block[:, d * width : (d + 1) * width]

        def send(which, outs, kept):
            packed, sems = kept
            copy = pltpu.make_async_copy(packed.at[:, which], outs[0].at[:, which], sems.at[which])
            copy.start()
            return [copy]

        def read(got_ref, out_ref):
            for d in range(near):
                out_ref[:, d * width : (d + 1) * width] = got_ref[d]

        (packed,) = pack(
            store,
            send,
            [shape(near, 3, rows, width)],
            rows,
            features,
            (query_rows, key_rows, value_rows, q_gain, k_gain),
            [pltpu.VMEM((near, 3, rows, width), BF16), pltpu.SemaphoreType.DMA((3,))],
        )
        own = exchange(packed, NEAR).reshape(outer, n_head, 3, rows, width)
        every = lax.all_gather(own, "inner")
        mixed = pl.pallas_call(
            functools.partial(gathered_kernel, outer, inner),
            grid=(outer, HEADS // near),
            in_specs=[
                pl.BlockSpec(memory_space=pltpu.SMEM),
                pl.BlockSpec((1, n_head, 1, rows, HDIM), lambda i, h: (i, 0, 0, 0, h)),
                pl.BlockSpec((inner, outer, n_head, 3, rows, HDIM), lambda i, h: (0, 0, 0, 0, 0, h)),
            ],
            out_specs=pl.BlockSpec((1, n_head, rows, HDIM), lambda i, h: (i, 0, 0, h)),
            out_shape=shape(outer, n_head, rows, width),
            scratch_shapes=[pltpu.VMEM((outer * inner, block, block), jnp.float32)],
            compiler_params=PARAMS,
            name="attend",
        )(tile_mask, own, every)
        return pl.pallas_call(
            read, out_shape=shape(rows, features), compiler_params=PARAMS, name="unpack"
        )(exchange(mixed.reshape(near, rows, width), NEAR))

    return per_device


def solution(mesh):
    n_blk, n_head = mesh.shape["blk"], mesh.shape["head"]
    outer = max(d for d in range(1, n_blk + 1) if n_blk % d == 0 and HEADS % (n_head * d) == 0)
    inner = n_blk // outer
    near, far = outer * n_head, n_blk * n_head

    def per_device(query_rows, *others):
        in_pairs = inner == 2 and n_head == 2 and mesh.shape["batch"] == 2 and near & (near - 1) == 0
        if in_pairs and HEADS == near + far and query_rows.shape[0] == TILE:
            return halved(far, near)(query_rows, *others)
        return gathered(outer, inner, n_head, near)(query_rows, *others)

    split = P(("batch", "outer", "inner", "head"), None)
    return jax.shard_map(
        per_device,
        mesh=Mesh(
            mesh.devices.reshape(outer, inner, n_head, mesh.shape["batch"]), ("outer", "inner", "head", "batch")
        ),
        in_specs=(split, split, split, P(), P(), P()),
        out_specs=split,
        check_vma=False,
    )
```

profile of v0, /device:TPU:0, one launch (start us, length us, event | category | flops | bytes accessed | tf_op | source)
XLA Modules:
  0.0 93.9 jit_solution(8760190887023050940)
XLA Ops:
  0.0 3.3 %pack.1 = (bf16[3,128,128]{2,1,0:T(8,128)(2,1)}, bf16[3,128,128]{2,1,0:T(8,128)(2,1)}, bf16[3,128,128]{2,1,0:T(8,128)(2,1)}, bf16[3,128,128]{2,1,0:T(8,128)(2,1)...) custom-call(bf16[128,3072]{1,0:T(8,128)(2,1)} %refs_0_.1, ...), custom_call_target="tpu_custom_call" | custom-call | tf_op jit(solution)/shard_map/pack/pallas_call | solution.py:71
  3.3 6.0 %collective-permute-start = (bf16[3,128,128]{2,1,0:T(8,128)(2,1)}, bf16[3,128,128]{2,1,0:T(8,128)(2,1)S(1)}, u32[]{:S(2)}, u32[]{:S(2)}) collective-permute-start(bf16[3,128,128]{2,1,0:T(8,128)(2,1)} %get-tuple-element.16), channel_id=1, source_target_pairs={{0,26},{1,11},{2,24},{3,9},{8,18},{9,3},{10,16},{11,1},{16,10},{17... | collective-permute-start | bytes 294920 | tf_op jit(solution)/shard_map/ppermute | solution.py:254
  9.3 0.0 collective-permute-start.1
  9.3 0.9 collective-permute-start.2
  10.2 1.1 %collective-permute-start.3 = (bf16[3,128,128]{2,1,0:T(8,128)(2,1)}, bf16[3,128,128]{2,1,0:T(8,128)(2,1)S(1)}, u32[]{:S(2)}, u32[]{:S(2)}) collective-permute-start(bf16[3,128,128]{2,1,0:T(8,128)(2,1)} %get-tuple-element.19), channel_id=1, source_target_pairs={{0,8},{1,25},{2,10},{3,27},{8,0},{9,17},{10,2},{11,19},{16,24},{17... | collective-permute-start | bytes 294920 | tf_op jit(solution)/shard_map/ppermute | solution.py:254
  11.3 2.8 %collective-permute-start.4 = (bf16[3,128,128]{2,1,0:T(8,128)(2,1)}, bf16[3,128,128]{2,1,0:T(8,128)(2,1)S(1)}, u32[]{:S(2)}, u32[]{:S(2)}) collective-permute-start(bf16[3,128,128]{2,1,0:T(8,128)(2,1)} %get-tuple-element.20), channel_id=1, source_target_pairs={{0,18},{1,3},{2,16},{3,1},{8,26},{9,11},{10,24},{11,9},{16,2},{17,... | collective-permute-start | bytes 294920 | tf_op jit(solution)/shard_map/ppermute | solution.py:254
  14.2 0.0 collective-permute-done.refs_0_
  14.2 1.0 %collective-permute-start.5 = (bf16[3,128,128]{2,1,0:T(8,128)(2,1)}, bf16[3,128,128]{2,1,0:T(8,128)(2,1)S(1)}, u32[]{:S(2)}, u32[]{:S(2)}) collective-permute-start(bf16[3,128,128]{2,1,0:T(8,128)(2,1)} %get-tuple-element.21), channel_id=1, source_target_pairs={{0,2},{1,19},{2,0},{3,17},{8,10},{9,27},{10,8},{11,25},{16,18},{17... | collective-permute-start | bytes 294920 | tf_op jit(solution)/shard_map/ppermute | solution.py:254
  15.2 0.7 collective-permute-done.1.refs_1_
  15.8 3.8 %collective-permute-start.6 = (bf16[3,128,128]{2,1,0:T(8,128)(2,1)}, bf16[3,128,128]{2,1,0:T(8,128)(2,1)S(1)}, u32[]{:S(2)}, u32[]{:S(2)}) collective-permute-start(bf16[3,128,128]{2,1,0:T(8,128)(2,1)} %get-tuple-element.22), channel_id=1, source_target_pairs={{0,16},{1,1},{2,18},{3,3},{8,24},{9,9},{10,26},{11,11},{16,0},{17,... | collective-permute-start | bytes 294920 | tf_op jit(solution)/shard_map/ppermute | solution.py:254
  19.6 0.0 collective-permute-done.2.refs_2_
  19.6 1.6 %collective-permute-start.7 = (bf16[3,128,128]{2,1,0:T(8,128)(2,1)}, bf16[3,128,128]{2,1,0:T(8,128)(2,1)S(1)}, u32[]{:S(2)}, u32[]{:S(2)}) collective-permute-start(bf16[3,128,128]{2,1,0:T(8,128)(2,1)} %get-tuple-element.23), channel_id=1, source_target_pairs={{0,0},{1,17},{2,2},{3,19},{8,8},{9,25},{10,10},{11,27},{16,16},{17... | collective-permute-start | bytes 294920 | tf_op jit(solution)/shard_map/ppermute | solution.py:254
  21.2 0.0 copy-start
  21.2 5.3 %all-to-all-start.1 = ((bf16[16,3,128,128]{3,2,1,0:T(8,128)(2,1)}), bf16[16,3,128,128]{3,2,1,0:T(8,128)(2,1)S(1)}, u32[]{:S(2)}, u32[]{:S(2)}) async-start(bf16[16,3,128,128]{3,2,1,0:T(8,128)(2,1)} %get-tuple-element.26), calls=%async_computation.1 | async-start | bytes 3145728 | tf_op jit(solution)/shard_map/all_to_all | solution.py:29
  26.5 0.0 collective-permute-done.3.refs_3_
  26.5 0.0 collective-permute-done.4.refs_4_
  26.5 0.0 collective-permute-done.5.refs_5_
  26.6 0.9 collective-permute-done.6.refs_6_
  27.5 0.0 collective-permute-done.7.refs_7_
  27.5 0.1 collect.1
  27.6 1.6 %collective-permute-start.8 = (bf16[2,1024,128]{2,1,0:T(8,128)(2,1)S(1)}, bf16[2,1024,128]{2,1,0:T(8,128)(2,1)S(1)}, u32[]{:S(2)}, u32[]{:S(2)}) collective-permute-start(bf16[2,1024,128]{2,1,0:T(8,128)(2,1)S(1)} %get-tuple-element.25.own_ref), channel_id=1, source_target_pairs={{0,4},{4,0},{1,5},{5,1},{2,6},{6,2},{3,7},{7,3},{8,12},{12,8},{9,1... | collective-permute-start | bytes 1572872 | tf_op jit(solution)/shard_map/ppermute | solution.py:306
  29.2 22.7 %collective-permute-done.8.other_ref = bf16[2,1024,128]{2,1,0:T(8,128)(2,1)S(1)} collective-permute-done((bf16[2,1024,128]{2,1,0:T(8,128)(2,1)S(1)}, bf16[2,1024,128]{2,1,0:T(8,128)(2,1)S(1)}, u32[]{:S(2)}, u32[]{:S(2)}) %collective-permute-start.8) | collective-permute-done | bytes 524320 | tf_op jit(solution)/shard_map/ppermute | solution.py:306
  51.9 0.0 copy-done
  51.9 4.5 %attend_shared.1.refs_0_ = bf16[1024,128]{1,0:T(8,128)(2,1)} custom-call(s32[16,16]{1,0:T(8,128)S(1)} %copy-done, bf16[1024,128]{1,0:T(8,128)(2,1)S(1)} %get-tuple-element.24.q_ref, bf16[2,1024,128]{2,1,0:T(8,128)(2,1)S(1)} %get-tuple-element.25.own_ref, bf16[2,1024,128]{2,1,0:T(8,128)(2,1)S(1)} %collective-permute-done.8.other_ref), custom_call_target="tpu_custom_call" | custom-call | flops 25769803776 | bytes 2097152 | tf_op jit(solution)/shard_map/attend_shared/pallas_call | solution.py:313
  56.4 2.4 %all-to-all-done.1.qkv_ref = bf16[16,3,128,128]{3,2,1,0:T(8,128)(2,1)S(1)} async-done(((bf16[16,3,128,128]{3,2,1,0:T(8,128)(2,1)}), bf16[16,3,128,128]{3,2,1,0:T(8,128)(2,1)S(1)}, u32[]{:S(2)}, u32[]{:S(2)}) %all-to-all-start.1) | async-done | bytes 1572896 | tf_op jit(solution)/shard_map/all_to_all | solution.py:29
  58.8 7.0 %all-to-all-start = ((bf16[8,128,128]{2,1,0:T(8,128)(2,1)}), bf16[8,128,128]{2,1,0:T(8,128)(2,1)S(1)}, u32[]{:S(2)}, u32[]{:S(2)}) async-start(bf16[8,128,128]{2,1,0:T(8,128)(2,1)} %bitcast.2), calls=%async_computation | async-start | bytes 524288 | tf_op jit(solution)/shard_map/all_to_all | solution.py:29
  65.8 6.3 %attend_whole.1 = bf16[16,128,128]{2,1,0:T(8,128)(2,1)S(1)} custom-call(s32[16,16]{1,0:T(8,128)S(1)} %copy-done, bf16[16,3,128,128]{3,2,1,0:T(8,128)(2,1)S(1)} %all-to-all-done.1.qkv_ref, bf16[1024,128]{1,0:T(8,128)(2,1)} %attend_shared.1.refs_0_), custom_call_target="tpu_custom_call" | custom-call | flops 8589934592 | bytes 4194304 | tf_op jit(solution)/shard_map/attend_whole/pallas_call | solution.py:323
  72.1 2.4 %all-to-all-done.shared = bf16[8,128,128]{2,1,0:T(8,128)(2,1)S(1)} async-done(((bf16[8,128,128]{2,1,0:T(8,128)(2,1)}), bf16[8,128,128]{2,1,0:T(8,128)(2,1)S(1)}, u32[]{:S(2)}, u32[]{:S(2)}) %all-to-all-start) | async-done | bytes 262176 | tf_op jit(solution)/shard_map/all_to_all | solution.py:29
  74.5 18.3 %all_to_all.15.whole = bf16[16,128,128]{2,1,0:T(8,128)(2,1)S(1)} all-to-all(bf16[16,128,128]{2,1,0:T(8,128)(2,1)S(1)} %attend_whole.1), channel_id=1, replica_groups=mesh['outer'=4,'inner'=2,'head'=2,'batch'=2] {'outer','inner','head'}, dimensions={0} | all-to-all | bytes 1048576 | tf_op jit(solution)/shard_map/all_to_all | solution.py:29
  92.9 1.1 %unpack.1 = bf16[128,3072]{1,0:T(8,128)(2,1)} custom-call(bf16[8,128,128]{2,1,0:T(8,128)(2,1)S(1)} %all-to-all-done.shared, bf16[16,128,128]{2,1,0:T(8,128)(2,1)S(1)} %all_to_all.15.whole), custom_call_target="tpu_custom_call" | custom-call | tf_op jit(solution)/shard_map/unpack/pallas_call | solution.py:333
Async XLA Ops:
  3.3 10.9 %collective-permute-start = (bf16[3,128,128]{2,1,0:T(8,128)(2,1)}, bf16[3,128,128]{2,1,0:T(8,128)(2,1)S(1)}, u32[]{:S(2)}, u32[]{:S(2)}) collective-permute-start(bf16[3,128,128]{2,1,0:T(8,128)(2,1)} %get-tuple-element.16), channel_id=1, source_target_pairs={{0,26},{1,11},{2,24},{3,9},{8,18},{9,3},{10,16},{11,1},{16,10},{17... | collective-permute-start | bytes 294920 | tf_op jit(solution)/shard_map/ppermute | solution.py:254
  9.3 6.5 %collective-permute-start.1 = (bf16[3,128,128]{2,1,0:T(8,128)(2,1)}, bf16[3,128,128]{2,1,0:T(8,128)(2,1)S(1)}, u32[]{:S(2)}, u32[]{:S(2)}) collective-permute-start(bf16[3,128,128]{2,1,0:T(8,128)(2,1)} %get-tuple-element.17), channel_id=1, source_target_pairs={{0,10},{1,27},{2,8},{3,25},{8,2},{9,19},{10,0},{11,17},{16,26},{17... | collective-permute-start | bytes 294920 | tf_op jit(solution)/shard_map/ppermute | solution.py:254
  9.3 10.3 %collective-permute-start.2 = (bf16[3,128,128]{2,1,0:T(8,128)(2,1)}, bf16[3,128,128]{2,1,0:T(8,128)(2,1)S(1)}, u32[]{:S(2)}, u32[]{:S(2)}) collective-permute-start(bf16[3,128,128]{2,1,0:T(8,128)(2,1)} %get-tuple-element.18), channel_id=1, source_target_pairs={{0,24},{1,9},{2,26},{3,11},{8,16},{9,1},{10,18},{11,3},{16,8},{17,... | collective-permute-start | bytes 294920 | tf_op jit(solution)/shard_map/ppermute | solution.py:254
  10.2 16.3 %collective-permute-start.3 = (bf16[3,128,128]{2,1,0:T(8,128)(2,1)}, bf16[3,128,128]{2,1,0:T(8,128)(2,1)S(1)}, u32[]{:S(2)}, u32[]{:S(2)}) collective-permute-start(bf16[3,128,128]{2,1,0:T(8,128)(2,1)} %get-tuple-element.19), channel_id=1, source_target_pairs={{0,8},{1,25},{2,10},{3,27},{8,0},{9,17},{10,2},{11,19},{16,24},{17... | collective-permute-start | bytes 294920 | tf_op jit(solution)/shard_map/ppermute | solution.py:254
  11.3 15.2 %collective-permute-start.4 = (bf16[3,128,128]{2,1,0:T(8,128)(2,1)}, bf16[3,128,128]{2,1,0:T(8,128)(2,1)S(1)}, u32[]{:S(2)}, u32[]{:S(2)}) collective-permute-start(bf16[3,128,128]{2,1,0:T(8,128)(2,1)} %get-tuple-element.20), channel_id=1, source_target_pairs={{0,18},{1,3},{2,16},{3,1},{8,26},{9,11},{10,24},{11,9},{16,2},{17,... | collective-permute-start | bytes 294920 | tf_op jit(solution)/shard_map/ppermute | solution.py:254
  14.2 12.4 %collective-permute-start.5 = (bf16[3,128,128]{2,1,0:T(8,128)(2,1)}, bf16[3,128,128]{2,1,0:T(8,128)(2,1)S(1)}, u32[]{:S(2)}, u32[]{:S(2)}) collective-permute-start(bf16[3,128,128]{2,1,0:T(8,128)(2,1)} %get-tuple-element.21), channel_id=1, source_target_pairs={{0,2},{1,19},{2,0},{3,17},{8,10},{9,27},{10,8},{11,25},{16,18},{17... | collective-permute-start | bytes 294920 | tf_op jit(solution)/shard_map/ppermute | solution.py:254
  15.8 11.6 %collective-permute-start.6 = (bf16[3,128,128]{2,1,0:T(8,128)(2,1)}, bf16[3,128,128]{2,1,0:T(8,128)(2,1)S(1)}, u32[]{:S(2)}, u32[]{:S(2)}) collective-permute-start(bf16[3,128,128]{2,1,0:T(8,128)(2,1)} %get-tuple-element.22), channel_id=1, source_target_pairs={{0,16},{1,1},{2,18},{3,3},{8,24},{9,9},{10,26},{11,11},{16,0},{17,... | collective-permute-start | bytes 294920 | tf_op jit(solution)/shard_map/ppermute | solution.py:254
  19.6 7.9 %collective-permute-start.7 = (bf16[3,128,128]{2,1,0:T(8,128)(2,1)}, bf16[3,128,128]{2,1,0:T(8,128)(2,1)S(1)}, u32[]{:S(2)}, u32[]{:S(2)}) collective-permute-start(bf16[3,128,128]{2,1,0:T(8,128)(2,1)} %get-tuple-element.23), channel_id=1, source_target_pairs={{0,0},{1,17},{2,2},{3,19},{8,8},{9,25},{10,10},{11,27},{16,16},{17... | collective-permute-start | bytes 294920 | tf_op jit(solution)/shard_map/ppermute | solution.py:254
  21.2 30.7 %copy-start = (s32[16,16]{1,0:T(8,128)S(1)}, s32[16,16]{1,0:T(8,128)}, u32[]{:S(2)}) copy-start(s32[16,16]{1,0:T(8,128)} %mask_ref.3) | copy-start | bytes 3076
  21.2 37.6 %all-to-all-start.1 = ((bf16[16,3,128,128]{3,2,1,0:T(8,128)(2,1)}), bf16[16,3,128,128]{3,2,1,0:T(8,128)(2,1)S(1)}, u32[]{:S(2)}, u32[]{:S(2)}) async-start(bf16[16,3,128,128]{3,2,1,0:T(8,128)(2,1)} %get-tuple-element.26), calls=%async_computation.1 | async-start | bytes 3145728 | tf_op jit(solution)/shard_map/all_to_all | solution.py:29
  27.6 24.3 %collective-permute-start.8 = (bf16[2,1024,128]{2,1,0:T(8,128)(2,1)S(1)}, bf16[2,1024,128]{2,1,0:T(8,128)(2,1)S(1)}, u32[]{:S(2)}, u32[]{:S(2)}) collective-permute-start(bf16[2,1024,128]{2,1,0:T(8,128)(2,1)S(1)} %get-tuple-element.25.own_ref), channel_id=1, source_target_pairs={{0,4},{4,0},{1,5},{5,1},{2,6},{6,2},{3,7},{7,3},{8,12},{12,8},{9,1... | collective-permute-start | bytes 1572872 | tf_op jit(solution)/shard_map/ppermute | solution.py:306
  58.8 15.7 %all-to-all-start = ((bf16[8,128,128]{2,1,0:T(8,128)(2,1)}), bf16[8,128,128]{2,1,0:T(8,128)(2,1)S(1)}, u32[]{:S(2)}, u32[]{:S(2)}) async-start(bf16[8,128,128]{2,1,0:T(8,128)(2,1)} %bitcast.2), calls=%async_computation | async-start | bytes 524288 | tf_op jit(solution)/shard_map/all_to_all | solution.py:29
where the time goes:
time: 94.4 us; the launch traced here: 93.9 us
  starting transfers between devices  31.1 us (33%)
  waiting for transfers between devices  29.2 us (31%)
  blocking collectives  18.3 us (19%)
  Pallas kernels  15.3 us (16%)
    ppermute x1, waiting for transfers between devices, per_device(): kv_other = lax.ppermute(kv_near, 'inner', [(0, 1), (1, 0)])  22.7 us
    all_to_all x1, blocking collectives, exchange(): return lax.all_to_all(x, axes, split_axis=0, concat_axis=0, tiled=True)  18.3 us
    ppermute x8, starting transfers between devices, swap(): return lax.ppermute(piece, (*NEAR, 'batch'), pairs)  17.2 us
    all_to_all x2, starting transfers between devices, exchange(): return lax.all_to_all(x, axes, split_axis=0, concat_axis=0, tiled=True)  12.3 us
    pallas_call x1, Pallas kernels, per_device(): pl.pallas_call(functools.partial(whole_kernel, far), in_specs=[smem, vmem...  6.34 us
    all_to_all x2, waiting for transfers between devices, exchange(): return lax.all_to_all(x, axes, split_axis=0, concat_axis=0, tiled=True)  4.83 us
    pallas_call x1, Pallas kernels, per_device(): pl.pallas_call(shared_kernel, in_specs=[smem] + [vmem] * 3, out_shape=sha...  4.47 us
    pallas_call x1, Pallas kernels, pack(): pl.pallas_call(kernel, in_specs=[hbm] * 5, out_specs=[hbm] * len(out_shap...  3.28 us
  transfers between devices with their start and end apart: 11, of which 5 were waited for; matrix products, arithmetic and copies ran while one was open for 0% of the time, Pallas kernels for 12%

commit v1 on v0

--- a/solution.py
+++ b/solution.py
@@ -246,7 +246,7 @@
 
 def halved(far, near):
     steps = []
-    for d in reversed(range(near // 2)):
+    for d in (*range(near // 4, near // 2), *reversed(range(near // 4))):
         steps += [(near // 2 + d, d), (d, near // 2 + d)]
 
     def swap(piece, step):

time: 94.4 us -> 92.2 us (0.977)
  waiting for transfers between devices: 29.2 us -> 23.9 us
  starting transfers between devices: 31.1 us -> 35 us
    ppermute x1, waiting for transfers between devices: 22.7 us -> 19 us  [per_device(): kv_other = lax.ppermute(kv_near, 'inner', [(0, 1), (1, 0)])]
    all_to_all x2, starting transfers between devices: 12.3 us -> 14.9 us  [exchange(): return lax.all_to_all(x, axes, split_axis=0, concat_axis=0, tiled=True)]
    ppermute x1, starting transfers between devices: 1.6 us -> 3.23 us  [per_device(): kv_other = lax.ppermute(kv_near, 'inner', [(0, 1), (1, 0)])]
    ppermute x8, waiting for transfers between devices: 1.59 us -> 0.02 us  [swap(): return lax.ppermute(piece, (*NEAR, 'batch'), pairs)]
  transfers between devices with their start and end apart: 11 -> 11, of which waited for: 5 -> 3; matrix products, arithmetic and copies ran while one was open for 0% -> 0% of each run, Pallas kernels for 12% -> 12%
where the time goes in v1:
time: 92.2 us; the launch traced here: 91.8 us
  starting transfers between devices  35 us (38%)
  waiting for transfers between devices  23.9 us (26%)
  blocking collectives  17.5 us (19%)
  Pallas kernels  15.3 us (17%)
    ppermute x1, waiting for transfers between devices, per_device(): kv_other = lax.ppermute(kv_near, 'inner', [(0, 1), (1, 0)])  19 us
    all_to_all x1, blocking collectives, exchange(): return lax.all_to_all(x, axes, split_axis=0, concat_axis=0, tiled=True)  17.5 us
    ppermute x8, starting transfers between devices, swap(): return lax.ppermute(piece, (*NEAR, 'batch'), pairs)  16.8 us
    all_to_all x2, starting transfers between devices, exchange(): return lax.all_to_all(x, axes, split_axis=0, concat_axis=0, tiled=True)  14.9 us
    pallas_call x1, Pallas kernels, per_device(): pl.pallas_call(functools.partial(whole_kernel, far), in_specs=[smem, vmem...  6.34 us
    all_to_all x2, waiting for transfers between devices, exchange(): return lax.all_to_all(x, axes, split_axis=0, concat_axis=0, tiled=True)  4.9 us
    pallas_call x1, Pallas kernels, per_device(): pl.pallas_call(shared_kernel, in_specs=[smem] + [vmem] * 3, out_shape=sha...  4.48 us
    pallas_call x1, Pallas kernels, pack(): pl.pallas_call(kernel, in_specs=[hbm] * 5, out_specs=[hbm] * len(out_shap...  3.28 us
  transfers between devices with their start and end apart: 11, of which 3 were waited for; matrix products, arithmetic and copies ran while one was open for 0% of the time, Pallas kernels for 12%

profile of v1, /device:TPU:0, one launch (start us, length us, event | category | flops | bytes accessed | tf_op | source)
XLA Modules:
  0.0 91.8 jit_solution(7440874283912876268)
XLA Ops:
  0.0 3.3 %pack.1 = (bf16[3,128,128]{2,1,0:T(8,128)(2,1)}, bf16[3,128,128]{2,1,0:T(8,128)(2,1)}, bf16[3,128,128]{2,1,0:T(8,128)(2,1)}, bf16[3,128,128]{2,1,0:T(8,128)(2,1)...) custom-call(bf16[128,3072]{1,0:T(8,128)(2,1)} %refs_0_.1, ...), custom_call_target="tpu_custom_call" | custom-call | tf_op jit(solution)/shard_map/pack/pallas_call | solution.py:71
  3.3 5.1 %collective-permute-start = (bf16[3,128,128]{2,1,0:T(8,128)(2,1)}, bf16[3,128,128]{2,1,0:T(8,128)(2,1)S(1)}, u32[]{:S(2)}, u32[]{:S(2)}) collective-permute-start(bf16[3,128,128]{2,1,0:T(8,128)(2,1)} %get-tuple-element.16), channel_id=1, source_target_pairs={{0,24},{1,9},{2,26},{3,11},{8,16},{9,1},{10,18},{11,3},{16,8},{17,... | collective-permute-start | bytes 294920 | tf_op jit(solution)/shard_map/ppermute | solution.py:254
  8.4 0.0 collective-permute-start.1
  8.4 1.8 %collective-permute-start.2 = (bf16[3,128,128]{2,1,0:T(8,128)(2,1)}, bf16[3,128,128]{2,1,0:T(8,128)(2,1)S(1)}, u32[]{:S(2)}, u32[]{:S(2)}) collective-permute-start(bf16[3,128,128]{2,1,0:T(8,128)(2,1)} %get-tuple-element.18), channel_id=1, source_target_pairs={{0,26},{1,11},{2,24},{3,9},{8,18},{9,3},{10,16},{11,1},{16,10},{17... | collective-permute-start | bytes 294920 | tf_op jit(solution)/shard_map/ppermute | solution.py:254
  10.2 1.1 %collective-permute-start.3 = (bf16[3,128,128]{2,1,0:T(8,128)(2,1)}, bf16[3,128,128]{2,1,0:T(8,128)(2,1)S(1)}, u32[]{:S(2)}, u32[]{:S(2)}) collective-permute-start(bf16[3,128,128]{2,1,0:T(8,128)(2,1)} %get-tuple-element.19), channel_id=1, source_target_pairs={{0,10},{1,27},{2,8},{3,25},{8,2},{9,19},{10,0},{11,17},{16,26},{17... | collective-permute-start | bytes 294920 | tf_op jit(solution)/shard_map/ppermute | solution.py:254
  11.4 3.3 %collective-permute-start.4 = (bf16[3,128,128]{2,1,0:T(8,128)(2,1)}, bf16[3,128,128]{2,1,0:T(8,128)(2,1)S(1)}, u32[]{:S(2)}, u32[]{:S(2)}) collective-permute-start(bf16[3,128,128]{2,1,0:T(8,128)(2,1)} %get-tuple-element.20), channel_id=1, source_target_pairs={{0,18},{1,3},{2,16},{3,1},{8,26},{9,11},{10,24},{11,9},{16,2},{17,... | collective-permute-start | bytes 294920 | tf_op jit(solution)/shard_map/ppermute | solution.py:254
  14.6 0.0 collective-permute-done.refs_0_
  14.6 0.5 collective-permute-start.5
  15.2 0.0 collective-permute-done.1.refs_1_
  15.2 3.4 %collective-permute-start.6 = (bf16[3,128,128]{2,1,0:T(8,128)(2,1)}, bf16[3,128,128]{2,1,0:T(8,128)(2,1)S(1)}, u32[]{:S(2)}, u32[]{:S(2)}) collective-permute-start(bf16[3,128,128]{2,1,0:T(8,128)(2,1)} %get-tuple-element.22), channel_id=1, source_target_pairs={{0,16},{1,1},{2,18},{3,3},{8,24},{9,9},{10,26},{11,11},{16,0},{17,... | collective-permute-start | bytes 294920 | tf_op jit(solution)/shard_map/ppermute | solution.py:254
  18.6 0.0 collective-permute-done.2.refs_2_
  18.6 1.6 %collective-permute-start.7 = (bf16[3,128,128]{2,1,0:T(8,128)(2,1)}, bf16[3,128,128]{2,1,0:T(8,128)(2,1)S(1)}, u32[]{:S(2)}, u32[]{:S(2)}) collective-permute-start(bf16[3,128,128]{2,1,0:T(8,128)(2,1)} %get-tuple-element.23), channel_id=1, source_target_pairs={{0,0},{1,17},{2,2},{3,19},{8,8},{9,25},{10,10},{11,27},{16,16},{17... | collective-permute-start | bytes 294920 | tf_op jit(solution)/shard_map/ppermute | solution.py:254
  20.2 0.0 copy-start
  20.2 9.1 %all-to-all-start.1 = ((bf16[16,3,128,128]{3,2,1,0:T(8,128)(2,1)}), bf16[16,3,128,128]{3,2,1,0:T(8,128)(2,1)S(1)}, u32[]{:S(2)}, u32[]{:S(2)}) async-start(bf16[16,3,128,128]{3,2,1,0:T(8,128)(2,1)} %get-tuple-element.26), calls=%async_computation.1 | async-start | bytes 3145728 | tf_op jit(solution)/shard_map/all_to_all | solution.py:29
  29.2 0.0 collective-permute-done.3.refs_3_
  29.2 0.0 collective-permute-done.4.refs_4_
  29.2 0.0 collective-permute-done.5.refs_5_
  29.3 0.0 collective-permute-done.6.refs_6_
  29.3 0.0 collective-permute-done.7.refs_7_
  29.3 0.1 collect.1
  29.4 3.2 %collective-permute-start.8 = (bf16[2,1024,128]{2,1,0:T(8,128)(2,1)S(1)}, bf16[2,1024,128]{2,1,0:T(8,128)(2,1)S(1)}, u32[]{:S(2)}, u32[]{:S(2)}) collective-permute-start(bf16[2,1024,128]{2,1,0:T(8,128)(2,1)S(1)} %get-tuple-element.25.own_ref), channel_id=1, source_target_pairs={{0,4},{4,0},{1,5},{5,1},{2,6},{6,2},{3,7},{7,3},{8,12},{12,8},{9,1... | collective-permute-start | bytes 1572872 | tf_op jit(solution)/shard_map/ppermute | solution.py:306
  32.6 19.0 %collective-permute-done.8.other_ref = bf16[2,1024,128]{2,1,0:T(8,128)(2,1)S(1)} collective-permute-done((bf16[2,1024,128]{2,1,0:T(8,128)(2,1)S(1)}, bf16[2,1024,128]{2,1,0:T(8,128)(2,1)S(1)}, u32[]{:S(2)}, u32[]{:S(2)}) %collective-permute-start.8) | collective-permute-done | bytes 524320 | tf_op jit(solution)/shard_map/ppermute | solution.py:306
  51.6 0.0 copy-done
  51.6 4.5 %attend_shared.1.refs_0_ = bf16[1024,128]{1,0:T(8,128)(2,1)} custom-call(s32[16,16]{1,0:T(8,128)S(1)} %copy-done, bf16[1024,128]{1,0:T(8,128)(2,1)S(1)} %get-tuple-element.24.q_ref, bf16[2,1024,128]{2,1,0:T(8,128)(2,1)S(1)} %get-tuple-element.25.own_ref, bf16[2,1024,128]{2,1,0:T(8,128)(2,1)S(1)} %collective-permute-done.8.other_ref), custom_call_target="tpu_custom_call" | custom-call | flops 25769803776 | bytes 2097152 | tf_op jit(solution)/shard_map/attend_shared/pallas_call | solution.py:313
  56.1 3.0 %all-to-all-done.1.qkv_ref = bf16[16,3,128,128]{3,2,1,0:T(8,128)(2,1)S(1)} async-done(((bf16[16,3,128,128]{3,2,1,0:T(8,128)(2,1)}), bf16[16,3,128,128]{3,2,1,0:T(8,128)(2,1)S(1)}, u32[]{:S(2)}, u32[]{:S(2)}) %all-to-all-start.1) | async-done | bytes 1572896 | tf_op jit(solution)/shard_map/all_to_all | solution.py:29
  59.1 5.8 %all-to-all-start = ((bf16[8,128,128]{2,1,0:T(8,128)(2,1)}), bf16[8,128,128]{2,1,0:T(8,128)(2,1)S(1)}, u32[]{:S(2)}, u32[]{:S(2)}) async-start(bf16[8,128,128]{2,1,0:T(8,128)(2,1)} %bitcast.2), calls=%async_computation | async-start | bytes 524288 | tf_op jit(solution)/shard_map/all_to_all | solution.py:29
  65.0 6.3 %attend_whole.1 = bf16[16,128,128]{2,1,0:T(8,128)(2,1)S(1)} custom-call(s32[16,16]{1,0:T(8,128)S(1)} %copy-done, bf16[16,3,128,128]{3,2,1,0:T(8,128)(2,1)S(1)} %all-to-all-done.1.qkv_ref, bf16[1024,128]{1,0:T(8,128)(2,1)} %attend_shared.1.refs_0_), custom_call_target="tpu_custom_call" | custom-call | flops 8589934592 | bytes 4194304 | tf_op jit(solution)/shard_map/attend_whole/pallas_call | solution.py:323
  71.3 1.9 %all-to-all-done.shared = bf16[8,128,128]{2,1,0:T(8,128)(2,1)S(1)} async-done(((bf16[8,128,128]{2,1,0:T(8,128)(2,1)}), bf16[8,128,128]{2,1,0:T(8,128)(2,1)S(1)}, u32[]{:S(2)}, u32[]{:S(2)}) %all-to-all-start) | async-done | bytes 262176 | tf_op jit(solution)/shard_map/all_to_all | solution.py:29
  73.2 17.5 %all_to_all.15.whole = bf16[16,128,128]{2,1,0:T(8,128)(2,1)S(1)} all-to-all(bf16[16,128,128]{2,1,0:T(8,128)(2,1)S(1)} %attend_whole.1), channel_id=1, replica_groups=mesh['outer'=4,'inner'=2,'head'=2,'batch'=2] {'outer','inner','head'}, dimensions={0} | all-to-all | bytes 1048576 | tf_op jit(solution)/shard_map/all_to_all | solution.py:29
  90.7 1.1 %unpack.1 = bf16[128,3072]{1,0:T(8,128)(2,1)} custom-call(bf16[8,128,128]{2,1,0:T(8,128)(2,1)S(1)} %all-to-all-done.shared, bf16[16,128,128]{2,1,0:T(8,128)(2,1)S(1)} %all_to_all.15.whole), custom_call_target="tpu_custom_call" | custom-call | tf_op jit(solution)/shard_map/unpack/pallas_call | solution.py:333
Async XLA Ops:
  3.3 11.3 %collective-permute-start = (bf16[3,128,128]{2,1,0:T(8,128)(2,1)}, bf16[3,128,128]{2,1,0:T(8,128)(2,1)S(1)}, u32[]{:S(2)}, u32[]{:S(2)}) collective-permute-start(bf16[3,128,128]{2,1,0:T(8,128)(2,1)} %get-tuple-element.16), channel_id=1, source_target_pairs={{0,24},{1,9},{2,26},{3,11},{8,16},{9,1},{10,18},{11,3},{16,8},{17,... | collective-permute-start | bytes 294920 | tf_op jit(solution)/shard_map/ppermute | solution.py:254
  8.4 6.8 %collective-permute-start.1 = (bf16[3,128,128]{2,1,0:T(8,128)(2,1)}, bf16[3,128,128]{2,1,0:T(8,128)(2,1)S(1)}, u32[]{:S(2)}, u32[]{:S(2)}) collective-permute-start(bf16[3,128,128]{2,1,0:T(8,128)(2,1)} %get-tuple-element.17), channel_id=1, source_target_pairs={{0,8},{1,25},{2,10},{3,27},{8,0},{9,17},{10,2},{11,19},{16,24},{17... | collective-permute-start | bytes 294920 | tf_op jit(solution)/shard_map/ppermute | solution.py:254
  8.4 10.2 %collective-permute-start.2 = (bf16[3,128,128]{2,1,0:T(8,128)(2,1)}, bf16[3,128,128]{2,1,0:T(8,128)(2,1)S(1)}, u32[]{:S(2)}, u32[]{:S(2)}) collective-permute-start(bf16[3,128,128]{2,1,0:T(8,128)(2,1)} %get-tuple-element.18), channel_id=1, source_target_pairs={{0,26},{1,11},{2,24},{3,9},{8,18},{9,3},{10,16},{11,1},{16,10},{17... | collective-permute-start | bytes 294920 | tf_op jit(solution)/shard_map/ppermute | solution.py:254
  10.2 19.0 %collective-permute-start.3 = (bf16[3,128,128]{2,1,0:T(8,128)(2,1)}, bf16[3,128,128]{2,1,0:T(8,128)(2,1)S(1)}, u32[]{:S(2)}, u32[]{:S(2)}) collective-permute-start(bf16[3,128,128]{2,1,0:T(8,128)(2,1)} %get-tuple-element.19), channel_id=1, source_target_pairs={{0,10},{1,27},{2,8},{3,25},{8,2},{9,19},{10,0},{11,17},{16,26},{17... | collective-permute-start | bytes 294920 | tf_op jit(solution)/shard_map/ppermute | solution.py:254
  11.4 17.9 %collective-permute-start.4 = (bf16[3,128,128]{2,1,0:T(8,128)(2,1)}, bf16[3,128,128]{2,1,0:T(8,128)(2,1)S(1)}, u32[]{:S(2)}, u32[]{:S(2)}) collective-permute-start(bf16[3,128,128]{2,1,0:T(8,128)(2,1)} %get-tuple-element.20), channel_id=1, source_target_pairs={{0,18},{1,3},{2,16},{3,1},{8,26},{9,11},{10,24},{11,9},{16,2},{17,... | collective-permute-start | bytes 294920 | tf_op jit(solution)/shard_map/ppermute | solution.py:254
  14.6 14.6 %collective-permute-start.5 = (bf16[3,128,128]{2,1,0:T(8,128)(2,1)}, bf16[3,128,128]{2,1,0:T(8,128)(2,1)S(1)}, u32[]{:S(2)}, u32[]{:S(2)}) collective-permute-start(bf16[3,128,128]{2,1,0:T(8,128)(2,1)} %get-tuple-element.21), channel_id=1, source_target_pairs={{0,2},{1,19},{2,0},{3,17},{8,10},{9,27},{10,8},{11,25},{16,18},{17... | collective-permute-start | bytes 294920 | tf_op jit(solution)/shard_map/ppermute | solution.py:254
  15.2 14.1 %collective-permute-start.6 = (bf16[3,128,128]{2,1,0:T(8,128)(2,1)}, bf16[3,128,128]{2,1,0:T(8,128)(2,1)S(1)}, u32[]{:S(2)}, u32[]{:S(2)}) collective-permute-start(bf16[3,128,128]{2,1,0:T(8,128)(2,1)} %get-tuple-element.22), channel_id=1, source_target_pairs={{0,16},{1,1},{2,18},{3,3},{8,24},{9,9},{10,26},{11,11},{16,0},{17,... | collective-permute-start | bytes 294920 | tf_op jit(solution)/shard_map/ppermute | solution.py:254
  18.6 10.7 %collective-permute-start.7 = (bf16[3,128,128]{2,1,0:T(8,128)(2,1)}, bf16[3,128,128]{2,1,0:T(8,128)(2,1)S(1)}, u32[]{:S(2)}, u32[]{:S(2)}) collective-permute-start(bf16[3,128,128]{2,1,0:T(8,128)(2,1)} %get-tuple-element.23), channel_id=1, source_target_pairs={{0,0},{1,17},{2,2},{3,19},{8,8},{9,25},{10,10},{11,27},{16,16},{17... | collective-permute-start | bytes 294920 | tf_op jit(solution)/shard_map/ppermute | solution.py:254
  20.2 31.5 %copy-start = (s32[16,16]{1,0:T(8,128)S(1)}, s32[16,16]{1,0:T(8,128)}, u32[]{:S(2)}) copy-start(s32[16,16]{1,0:T(8,128)} %mask_ref.3) | copy-start | bytes 3076
  20.2 39.0 %all-to-all-start.1 = ((bf16[16,3,128,128]{3,2,1,0:T(8,128)(2,1)}), bf16[16,3,128,128]{3,2,1,0:T(8,128)(2,1)S(1)}, u32[]{:S(2)}, u32[]{:S(2)}) async-start(bf16[16,3,128,128]{3,2,1,0:T(8,128)(2,1)} %get-tuple-element.26), calls=%async_computation.1 | async-start | bytes 3145728 | tf_op jit(solution)/shard_map/all_to_all | solution.py:29
  29.4 22.2 %collective-permute-start.8 = (bf16[2,1024,128]{2,1,0:T(8,128)(2,1)S(1)}, bf16[2,1024,128]{2,1,0:T(8,128)(2,1)S(1)}, u32[]{:S(2)}, u32[]{:S(2)}) collective-permute-start(bf16[2,1024,128]{2,1,0:T(8,128)(2,1)S(1)} %get-tuple-element.25.own_ref), channel_id=1, source_target_pairs={{0,4},{4,0},{1,5},{5,1},{2,6},{6,2},{3,7},{7,3},{8,12},{12,8},{9,1... | collective-permute-start | bytes 1572872 | tf_op jit(solution)/shard_map/ppermute | solution.py:306
  59.1 14.1 %all-to-all-start = ((bf16[8,128,128]{2,1,0:T(8,128)(2,1)}), bf16[8,128,128]{2,1,0:T(8,128)(2,1)S(1)}, u32[]{:S(2)}, u32[]{:S(2)}) async-start(bf16[8,128,128]{2,1,0:T(8,128)(2,1)} %bitcast.2), calls=%async_computation | async-start | bytes 524288 | tf_op jit(solution)/shard_map/all_to_all | solution.py:29

commit v2 on v1

--- a/solution.py
+++ b/solution.py
@@ -247,7 +247,7 @@
 def halved(far, near):
     steps = []
     for d in (*range(near // 4, near // 2), *reversed(range(near // 4))):
-        steps += [(near // 2 + d, d), (d, near // 2 + d)]
+        steps += [(d, near // 2 + d), (near // 2 + d, d)]
 
     def swap(piece, step):
         pairs = [(2 * i + b, 2 * (i ^ step[b]) + b) for i in range(near) for b in range(2)]

time: 92.2 us -> 94.7 us (1.027)
  waiting for transfers between devices: 23.9 us -> 30.5 us
  starting transfers between devices: 35 us -> 30.2 us
    ppermute x1, waiting for transfers between devices: 19 us -> 22.3 us  [per_device(): kv_other = lax.ppermute(kv_near, 'inner', [(0, 1), (1, 0)])]
    ppermute x8, waiting for transfers between devices: 0.02 us -> 3.24 us  [swap(): return lax.ppermute(piece, (*NEAR, 'batch'), pairs)]
    ppermute x1, starting transfers between devices: 3.23 us -> 1.59 us  [per_device(): kv_other = lax.ppermute(kv_near, 'inner', [(0, 1), (1, 0)])]
    all_to_all x2, starting transfers between devices: 14.9 us -> 13.3 us  [exchange(): return lax.all_to_all(x, axes, split_axis=0, concat_axis=0, tiled=True)]
    ppermute x8, starting transfers between devices: 16.8 us -> 15.3 us  [swap(): return lax.ppermute(piece, (*NEAR, 'batch'), pairs)]
  transfers between devices with their start and end apart: 11 -> 11, of which waited for: 3 -> 5; matrix products, arithmetic and copies ran while one was open for 0% -> 0% of each run, Pallas kernels for 12% -> 12%
where the time goes in v2:
time: 94.7 us; the launch traced here: 94.2 us
  waiting for transfers between devices  30.5 us (32%)
  starting transfers between devices  30.2 us (32%)
  blocking collectives  18.2 us (19%)
  Pallas kernels  15.2 us (16%)
    ppermute x1, waiting for transfers between devices, per_device(): kv_other = lax.ppermute(kv_near, 'inner', [(0, 1), (1, 0)])  22.3 us
    all_to_all x1, blocking collectives, exchange(): return lax.all_to_all(x, axes, split_axis=0, concat_axis=0, tiled=True)  18.2 us
    ppermute x8, starting transfers between devices, swap(): return lax.ppermute(piece, (*NEAR, 'batch'), pairs)  15.3 us
    all_to_all x2, starting transfers between devices, exchange(): return lax.all_to_all(x, axes, split_axis=0, concat_axis=0, tiled=True)  13.3 us
    pallas_call x1, Pallas kernels, per_device(): pl.pallas_call(functools.partial(whole_kernel, far), in_specs=[smem, vmem...  6.33 us
    all_to_all x2, waiting for transfers between devices, exchange(): return lax.all_to_all(x, axes, split_axis=0, concat_axis=0, tiled=True)  5.03 us
    pallas_call x1, Pallas kernels, per_device(): pl.pallas_call(shared_kernel, in_specs=[smem] + [vmem] * 3, out_shape=sha...  4.47 us
    pallas_call x1, Pallas kernels, pack(): pl.pallas_call(kernel, in_specs=[hbm] * 5, out_specs=[hbm] * len(out_shap...  3.28 us
  transfers between devices with their start and end apart: 11, of which 5 were waited for; matrix products, arithmetic and copies ran while one was open for 0% of the time, Pallas kernels for 12%

profile of v2, /device:TPU:0, one launch (start us, length us, event | category | flops | bytes accessed | tf_op | source)
XLA Modules:
  0.0 94.2 jit_solution(11724049491494246608)
XLA Ops:
  0.0 3.3 %pack.1 = (bf16[3,128,128]{2,1,0:T(8,128)(2,1)}, bf16[3,128,128]{2,1,0:T(8,128)(2,1)}, bf16[3,128,128]{2,1,0:T(8,128)(2,1)}, bf16[3,128,128]{2,1,0:T(8,128)(2,1)...) custom-call(bf16[128,3072]{1,0:T(8,128)(2,1)} %refs_0_.1, ...), custom_call_target="tpu_custom_call" | custom-call | tf_op jit(solution)/shard_map/pack/pallas_call | solution.py:71
  3.3 3.1 %collective-permute-start = (bf16[3,128,128]{2,1,0:T(8,128)(2,1)}, bf16[3,128,128]{2,1,0:T(8,128)(2,1)S(1)}, u32[]{:S(2)}, u32[]{:S(2)}) collective-permute-start(bf16[3,128,128]{2,1,0:T(8,128)(2,1)} %get-tuple-element.16), channel_id=1, source_target_pairs={{0,8},{1,25},{2,10},{3,27},{8,0},{9,17},{10,2},{11,19},{16,24},{17... | collective-permute-start | bytes 294920 | tf_op jit(solution)/shard_map/ppermute | solution.py:254
  6.4 2.5 %collective-permute-start.1 = (bf16[3,128,128]{2,1,0:T(8,128)(2,1)}, bf16[3,128,128]{2,1,0:T(8,128)(2,1)S(1)}, u32[]{:S(2)}, u32[]{:S(2)}) collective-permute-start(bf16[3,128,128]{2,1,0:T(8,128)(2,1)} %get-tuple-element.17), channel_id=1, source_target_pairs={{0,24},{1,9},{2,26},{3,11},{8,16},{9,1},{10,18},{11,3},{16,8},{17,... | collective-permute-start | bytes 294920 | tf_op jit(solution)/shard_map/ppermute | solution.py:254
  8.9 1.6 %collective-permute-start.2 = (bf16[3,128,128]{2,1,0:T(8,128)(2,1)}, bf16[3,128,128]{2,1,0:T(8,128)(2,1)S(1)}, u32[]{:S(2)}, u32[]{:S(2)}) collective-permute-start(bf16[3,128,128]{2,1,0:T(8,128)(2,1)} %get-tuple-element.18), channel_id=1, source_target_pairs={{0,10},{1,27},{2,8},{3,25},{8,2},{9,19},{10,0},{11,17},{16,26},{17... | collective-permute-start | bytes 294920 | tf_op jit(solution)/shard_map/ppermute | solution.py:254
  10.5 0.9 collective-permute-start.3
  11.3 1.5 %collective-permute-start.4 = (bf16[3,128,128]{2,1,0:T(8,128)(2,1)}, bf16[3,128,128]{2,1,0:T(8,128)(2,1)S(1)}, u32[]{:S(2)}, u32[]{:S(2)}) collective-permute-start(bf16[3,128,128]{2,1,0:T(8,128)(2,1)} %get-tuple-element.20), channel_id=1, source_target_pairs={{0,2},{1,19},{2,0},{3,17},{8,10},{9,27},{10,8},{11,25},{16,18},{17... | collective-permute-start | bytes 294920 | tf_op jit(solution)/shard_map/ppermute | solution.py:254
  12.8 0.0 collective-permute-done.refs_0_
  12.8 1.9 %collective-permute-start.5 = (bf16[3,128,128]{2,1,0:T(8,128)(2,1)}, bf16[3,128,128]{2,1,0:T(8,128)(2,1)S(1)}, u32[]{:S(2)}, u32[]{:S(2)}) collective-permute-start(bf16[3,128,128]{2,1,0:T(8,128)(2,1)} %get-tuple-element.21), channel_id=1, source_target_pairs={{0,18},{1,3},{2,16},{3,1},{8,26},{9,11},{10,24},{11,9},{16,2},{17,... | collective-permute-start | bytes 294920 | tf_op jit(solution)/shard_map/ppermute | solution.py:254
  14.7 0.0 collective-permute-done.1.refs_1_
  14.7 1.5 %collective-permute-start.6 = (bf16[3,128,128]{2,1,0:T(8,128)(2,1)}, bf16[3,128,128]{2,1,0:T(8,128)(2,1)S(1)}, u32[]{:S(2)}, u32[]{:S(2)}) collective-permute-start(bf16[3,128,128]{2,1,0:T(8,128)(2,1)} %get-tuple-element.22), channel_id=1, source_target_pairs={{0,0},{1,17},{2,2},{3,19},{8,8},{9,25},{10,10},{11,27},{16,16},{17... | collective-permute-start | bytes 294920 | tf_op jit(solution)/shard_map/ppermute | solution.py:254
  16.3 2.2 %collective-permute-done.2.refs_2_ = bf16[3,128,128]{2,1,0:T(8,128)(2,1)S(1)} collective-permute-done((bf16[3,128,128]{2,1,0:T(8,128)(2,1)}, bf16[3,128,128]{2,1,0:T(8,128)(2,1)S(1)}, u32[]{:S(2)}, u32[]{:S(2)}) %collective-permute-start.2) | collective-permute-done | bytes 98336 | tf_op jit(solution)/shard_map/ppermute | solution.py:254
  18.5 2.3 %collective-permute-start.7 = (bf16[3,128,128]{2,1,0:T(8,128)(2,1)}, bf16[3,128,128]{2,1,0:T(8,128)(2,1)S(1)}, u32[]{:S(2)}, u32[]{:S(2)}) collective-permute-start(bf16[3,128,128]{2,1,0:T(8,128)(2,1)} %get-tuple-element.23), channel_id=1, source_target_pairs={{0,16},{1,1},{2,18},{3,3},{8,24},{9,9},{10,26},{11,11},{16,0},{17,... | collective-permute-start | bytes 294920 | tf_op jit(solution)/shard_map/ppermute | solution.py:254
  20.9 0.0 copy-start
  20.9 4.9 %all-to-all-start.1 = ((bf16[16,3,128,128]{3,2,1,0:T(8,128)(2,1)}), bf16[16,3,128,128]{3,2,1,0:T(8,128)(2,1)S(1)}, u32[]{:S(2)}, u32[]{:S(2)}) async-start(bf16[16,3,128,128]{3,2,1,0:T(8,128)(2,1)} %get-tuple-element.26), calls=%async_computation.1 | async-start | bytes 3145728 | tf_op jit(solution)/shard_map/all_to_all | solution.py:29
  25.8 0.0 collective-permute-done.3.refs_3_
  25.8 0.0 collective-permute-done.4.refs_4_
  25.8 0.0 collective-permute-done.5.refs_5_
  25.8 0.0 collective-permute-done.6.refs_6_
  25.8 1.0 %collective-permute-done.7.refs_7_ = bf16[3,128,128]{2,1,0:T(8,128)(2,1)S(1)} collective-permute-done((bf16[3,128,128]{2,1,0:T(8,128)(2,1)}, bf16[3,128,128]{2,1,0:T(8,128)(2,1)S(1)}, u32[]{:S(2)}, u32[]{:S(2)}) %collective-permute-start.7) | collective-permute-done | bytes 98336 | tf_op jit(solution)/shard_map/ppermute | solution.py:254
  26.8 0.1 collect.1
  26.9 1.6 %collective-permute-start.8 = (bf16[2,1024,128]{2,1,0:T(8,128)(2,1)S(1)}, bf16[2,1024,128]{2,1,0:T(8,128)(2,1)S(1)}, u32[]{:S(2)}, u32[]{:S(2)}) collective-permute-start(bf16[2,1024,128]{2,1,0:T(8,128)(2,1)S(1)} %get-tuple-element.25.own_ref), channel_id=1, source_target_pairs={{0,4},{4,0},{1,5},{5,1},{2,6},{6,2},{3,7},{7,3},{8,12},{12,8},{9,1... | collective-permute-start | bytes 1572872 | tf_op jit(solution)/shard_map/ppermute | solution.py:306
  28.5 22.3 %collective-permute-done.8.other_ref = bf16[2,1024,128]{2,1,0:T(8,128)(2,1)S(1)} collective-permute-done((bf16[2,1024,128]{2,1,0:T(8,128)(2,1)S(1)}, bf16[2,1024,128]{2,1,0:T(8,128)(2,1)S(1)}, u32[]{:S(2)}, u32[]{:S(2)}) %collective-permute-start.8) | collective-permute-done | bytes 524320 | tf_op jit(solution)/shard_map/ppermute | solution.py:306
  50.7 0.0 copy-done
  50.7 4.5 %attend_shared.1.refs_0_ = bf16[1024,128]{1,0:T(8,128)(2,1)} custom-call(s32[16,16]{1,0:T(8,128)S(1)} %copy-done, bf16[1024,128]{1,0:T(8,128)(2,1)S(1)} %get-tuple-element.24.q_ref, bf16[2,1024,128]{2,1,0:T(8,128)(2,1)S(1)} %get-tuple-element.25.own_ref, bf16[2,1024,128]{2,1,0:T(8,128)(2,1)S(1)} %collective-permute-done.8.other_ref), custom_call_target="tpu_custom_call" | custom-call | flops 25769803776 | bytes 2097152 | tf_op jit(solution)/shard_map/attend_shared/pallas_call | solution.py:313
  55.2 2.8 %all-to-all-done.1.qkv_ref = bf16[16,3,128,128]{3,2,1,0:T(8,128)(2,1)S(1)} async-done(((bf16[16,3,128,128]{3,2,1,0:T(8,128)(2,1)}), bf16[16,3,128,128]{3,2,1,0:T(8,128)(2,1)S(1)}, u32[]{:S(2)}, u32[]{:S(2)}) %all-to-all-start.1) | async-done | bytes 1572896 | tf_op jit(solution)/shard_map/all_to_all | solution.py:29
  58.0 8.4 %all-to-all-start = ((bf16[8,128,128]{2,1,0:T(8,128)(2,1)}), bf16[8,128,128]{2,1,0:T(8,128)(2,1)S(1)}, u32[]{:S(2)}, u32[]{:S(2)}) async-start(bf16[8,128,128]{2,1,0:T(8,128)(2,1)} %bitcast.2), calls=%async_computation | async-start | bytes 524288 | tf_op jit(solution)/shard_map/all_to_all | solution.py:29
  66.4 6.3 %attend_whole.1 = bf16[16,128,128]{2,1,0:T(8,128)(2,1)S(1)} custom-call(s32[16,16]{1,0:T(8,128)S(1)} %copy-done, bf16[16,3,128,128]{3,2,1,0:T(8,128)(2,1)S(1)} %all-to-all-done.1.qkv_ref, bf16[1024,128]{1,0:T(8,128)(2,1)} %attend_shared.1.refs_0_), custom_call_target="tpu_custom_call" | custom-call | flops 8589934592 | bytes 4194304 | tf_op jit(solution)/shard_map/attend_whole/pallas_call | solution.py:323
  72.7 2.2 %all-to-all-done.shared = bf16[8,128,128]{2,1,0:T(8,128)(2,1)S(1)} async-done(((bf16[8,128,128]{2,1,0:T(8,128)(2,1)}), bf16[8,128,128]{2,1,0:T(8,128)(2,1)S(1)}, u32[]{:S(2)}, u32[]{:S(2)}) %all-to-all-start) | async-done | bytes 262176 | tf_op jit(solution)/shard_map/all_to_all | solution.py:29
  75.0 18.2 %all_to_all.15.whole = bf16[16,128,128]{2,1,0:T(8,128)(2,1)S(1)} all-to-all(bf16[16,128,128]{2,1,0:T(8,128)(2,1)S(1)} %attend_whole.1), channel_id=1, replica_groups=mesh['outer'=4,'inner'=2,'head'=2,'batch'=2] {'outer','inner','head'}, dimensions={0} | all-to-all | bytes 1048576 | tf_op jit(solution)/shard_map/all_to_all | solution.py:29
  93.1 1.1 %unpack.1 = bf16[128,3072]{1,0:T(8,128)(2,1)} custom-call(bf16[8,128,128]{2,1,0:T(8,128)(2,1)S(1)} %all-to-all-done.shared, bf16[16,128,128]{2,1,0:T(8,128)(2,1)S(1)} %all_to_all.15.whole), custom_call_target="tpu_custom_call" | custom-call | tf_op jit(solution)/shard_map/unpack/pallas_call | solution.py:333
Async XLA Ops:
  3.3 9.5 %collective-permute-start = (bf16[3,128,128]{2,1,0:T(8,128)(2,1)}, bf16[3,128,128]{2,1,0:T(8,128)(2,1)S(1)}, u32[]{:S(2)}, u32[]{:S(2)}) collective-permute-start(bf16[3,128,128]{2,1,0:T(8,128)(2,1)} %get-tuple-element.16), channel_id=1, source_target_pairs={{0,8},{1,25},{2,10},{3,27},{8,0},{9,17},{10,2},{11,19},{16,24},{17... | collective-permute-start | bytes 294920 | tf_op jit(solution)/shard_map/ppermute | solution.py:254
  6.4 8.3 %collective-permute-start.1 = (bf16[3,128,128]{2,1,0:T(8,128)(2,1)}, bf16[3,128,128]{2,1,0:T(8,128)(2,1)S(1)}, u32[]{:S(2)}, u32[]{:S(2)}) collective-permute-start(bf16[3,128,128]{2,1,0:T(8,128)(2,1)} %get-tuple-element.17), channel_id=1, source_target_pairs={{0,24},{1,9},{2,26},{3,11},{8,16},{9,1},{10,18},{11,3},{16,8},{17,... | collective-permute-start | bytes 294920 | tf_op jit(solution)/shard_map/ppermute | solution.py:254
  8.9 9.6 %collective-permute-start.2 = (bf16[3,128,128]{2,1,0:T(8,128)(2,1)}, bf16[3,128,128]{2,1,0:T(8,128)(2,1)S(1)}, u32[]{:S(2)}, u32[]{:S(2)}) collective-permute-start(bf16[3,128,128]{2,1,0:T(8,128)(2,1)} %get-tuple-element.18), channel_id=1, source_target_pairs={{0,10},{1,27},{2,8},{3,25},{8,2},{9,19},{10,0},{11,17},{16,26},{17... | collective-permute-start | bytes 294920 | tf_op jit(solution)/shard_map/ppermute | solution.py:254
  10.5 15.3 %collective-permute-start.3 = (bf16[3,128,128]{2,1,0:T(8,128)(2,1)}, bf16[3,128,128]{2,1,0:T(8,128)(2,1)S(1)}, u32[]{:S(2)}, u32[]{:S(2)}) collective-permute-start(bf16[3,128,128]{2,1,0:T(8,128)(2,1)} %get-tuple-element.19), channel_id=1, source_target_pairs={{0,26},{1,11},{2,24},{3,9},{8,18},{9,3},{10,16},{11,1},{16,10},{17... | collective-permute-start | bytes 294920 | tf_op jit(solution)/shard_map/ppermute | solution.py:254
  11.3 14.4 %collective-permute-start.4 = (bf16[3,128,128]{2,1,0:T(8,128)(2,1)}, bf16[3,128,128]{2,1,0:T(8,128)(2,1)S(1)}, u32[]{:S(2)}, u32[]{:S(2)}) collective-permute-start(bf16[3,128,128]{2,1,0:T(8,128)(2,1)} %get-tuple-element.20), channel_id=1, source_target_pairs={{0,2},{1,19},{2,0},{3,17},{8,10},{9,27},{10,8},{11,25},{16,18},{17... | collective-permute-start | bytes 294920 | tf_op jit(solution)/shard_map/ppermute | solution.py:254
  12.8 13.0 %collective-permute-start.5 = (bf16[3,128,128]{2,1,0:T(8,128)(2,1)}, bf16[3,128,128]{2,1,0:T(8,128)(2,1)S(1)}, u32[]{:S(2)}, u32[]{:S(2)}) collective-permute-start(bf16[3,128,128]{2,1,0:T(8,128)(2,1)} %get-tuple-element.21), channel_id=1, source_target_pairs={{0,18},{1,3},{2,16},{3,1},{8,26},{9,11},{10,24},{11,9},{16,2},{17,... | collective-permute-start | bytes 294920 | tf_op jit(solution)/shard_map/ppermute | solution.py:254
  14.7 11.1 %collective-permute-start.6 = (bf16[3,128,128]{2,1,0:T(8,128)(2,1)}, bf16[3,128,128]{2,1,0:T(8,128)(2,1)S(1)}, u32[]{:S(2)}, u32[]{:S(2)}) collective-permute-start(bf16[3,128,128]{2,1,0:T(8,128)(2,1)} %get-tuple-element.22), channel_id=1, source_target_pairs={{0,0},{1,17},{2,2},{3,19},{8,8},{9,25},{10,10},{11,27},{16,16},{17... | collective-permute-start | bytes 294920 | tf_op jit(solution)/shard_map/ppermute | solution.py:254
  18.5 8.3 %collective-permute-start.7 = (bf16[3,128,128]{2,1,0:T(8,128)(2,1)}, bf16[3,128,128]{2,1,0:T(8,128)(2,1)S(1)}, u32[]{:S(2)}, u32[]{:S(2)}) collective-permute-start(bf16[3,128,128]{2,1,0:T(8,128)(2,1)} %get-tuple-element.23), channel_id=1, source_target_pairs={{0,16},{1,1},{2,18},{3,3},{8,24},{9,9},{10,26},{11,11},{16,0},{17,... | collective-permute-start | bytes 294920 | tf_op jit(solution)/shard_map/ppermute | solution.py:254
  20.9 29.9 %copy-start = (s32[16,16]{1,0:T(8,128)S(1)}, s32[16,16]{1,0:T(8,128)}, u32[]{:S(2)}) copy-start(s32[16,16]{1,0:T(8,128)} %mask_ref.3) | copy-start | bytes 3076
  20.9 37.1 %all-to-all-start.1 = ((bf16[16,3,128,128]{3,2,1,0:T(8,128)(2,1)}), bf16[16,3,128,128]{3,2,1,0:T(8,128)(2,1)S(1)}, u32[]{:S(2)}, u32[]{:S(2)}) async-start(bf16[16,3,128,128]{3,2,1,0:T(8,128)(2,1)} %get-tuple-element.26), calls=%async_computation.1 | async-start | bytes 3145728 | tf_op jit(solution)/shard_map/all_to_all | solution.py:29
  26.9 23.9 %collective-permute-start.8 = (bf16[2,1024,128]{2,1,0:T(8,128)(2,1)S(1)}, bf16[2,1024,128]{2,1,0:T(8,128)(2,1)S(1)}, u32[]{:S(2)}, u32[]{:S(2)}) collective-permute-start(bf16[2,1024,128]{2,1,0:T(8,128)(2,1)S(1)} %get-tuple-element.25.own_ref), channel_id=1, source_target_pairs={{0,4},{4,0},{1,5},{5,1},{2,6},{6,2},{3,7},{7,3},{8,12},{12,8},{9,1... | collective-permute-start | bytes 1572872 | tf_op jit(solution)/shard_map/ppermute | solution.py:306
  58.0 17.0 %all-to-all-start = ((bf16[8,128,128]{2,1,0:T(8,128)(2,1)}), bf16[8,128,128]{2,1,0:T(8,128)(2,1)S(1)}, u32[]{:S(2)}, u32[]{:S(2)}) async-start(bf16[8,128,128]{2,1,0:T(8,128)(2,1)} %bitcast.2), calls=%async_computation | async-start | bytes 524288 | tf_op jit(solution)/shard_map/all_to_all | solution.py:29
